TPU v7x, 256 devices: a whole 4x4x8 slice. The times are simulated.
256 devices in a mesh: rows: 32 (over y_hi, z, core), cols: 8 (over y_lo, x).
Axes of the slice: x: 4, y: 4 (y_hi: 2, y_lo: 2; y = y_hi * 2 + y_lo), z: 8, core: 2. Of those that a mesh axis runs over, the one named last changes fastest.
Arguments:
- grid: bfloat16 [512, 512, 512], P('rows', 'cols'), may hold values from -9 to 9
- gain_lon: float32 [512], replicated, may hold values from 0.25 to 1.75
- qkv_lon: bfloat16 [512, 1536], replicated, may hold values from -1 to 1
- out_lon: bfloat16 [512, 512], replicated, may hold values from -0.25 to 0.25
- gain_lat: float32 [512], replicated, may hold values from 0.25 to 1.75
- qkv_lat: bfloat16 [512, 1536], replicated, may hold values from -1 to 1
- out_lat: bfloat16 [512, 512], replicated, may hold values from -0.25 to 0.25
Outputs:
- updated: bfloat16 [512, 512, 512], P('rows', 'cols')
All inputs are finite; a program needn't handle non-finite values.
Results may differ from a plain program's by a relative error of at most 0.009.
Values may be sent and summed in bfloat16 or wider, within the bound.
A program may use at most 64 MiB of HBM per device.

v0:
```python
import jax
import jax.numpy as jnp
from jax import lax
from jax.sharding import PartitionSpec as P

HEADS = 8


def norm_rows(u, gain):
    values = u.astype(jnp.float32)
    scale = lax.rsqrt(jnp.mean(values * values, axis=-1, keepdims=True) + 1e-06)
    return (values * scale * gain).astype(jnp.bfloat16)


def attend(proj, seq_first):
    width = proj.shape[-1] // 3
    head_size = width // HEADS
    lead = proj.shape[:2]
    query = proj[..., :width].reshape(lead + (HEADS, head_size))
    keys = proj[..., width : 2 * width].reshape(lead + (HEADS, head_size))
    values = proj[..., 2 * width :].reshape(lead + (HEADS, head_size))
    if seq_first:
        scores = jnp.einsum("qlhd,klhd->lhqk", query, keys, preferred_element_type=jnp.float32)
    else:
        scores = jnp.einsum("lqhd,lkhd->lhqk", query, keys, preferred_element_type=jnp.float32)
    scores = scores * head_size ** (-0.5)
    weights = jax.nn.softmax(scores, axis=-1).astype(jnp.bfloat16)
    if seq_first:
        mixed = jnp.einsum("lhqk,klhd->qlhd", weights, values, preferred_element_type=jnp.float32)
    else:
        mixed = jnp.einsum("lhqk,lkhd->lqhd", weights, values, preferred_element_type=jnp.float32)
    return mixed.astype(jnp.bfloat16).reshape(lead + (width,))


def project(normed, w_qkv):
    return jnp.dot(normed, w_qkv, preferred_element_type=jnp.float32).astype(jnp.bfloat16)


def finish(base, mixed, w_out):
    total = base.astype(jnp.float32) + jnp.dot(mixed, w_out, preferred_element_type=jnp.float32)
    return total.astype(jnp.bfloat16)


def per_device(grid, gain_lon, qkv_lon, out_lon, gain_lat, qkv_lat, out_lat):
    normed = norm_rows(grid, gain_lon)
    lines = lax.all_to_all(
        project(normed, qkv_lon), "cols", split_axis=0, concat_axis=1, tiled=True
    )
    mixed = attend(lines, False)
    back = lax.all_to_all(mixed, "cols", split_axis=1, concat_axis=0, tiled=True)
    first = finish(grid, back, out_lon)
    normed = norm_rows(first, gain_lat)
    columns = lax.all_to_all(
        project(normed, qkv_lat), "rows", split_axis=1, concat_axis=0, tiled=True
    )
    mixed = attend(columns, True)
    back = lax.all_to_all(mixed, "rows", split_axis=0, concat_axis=1, tiled=True)
    return finish(first, back, out_lat)


def solution(mesh):
    return jax.shard_map(
        per_device,
        mesh=mesh,
        in_specs=(P("rows", "cols", None), P(), P(), P(), P(), P(), P()),
        out_specs=P("rows", "cols", None),
        check_vma=False,
    )
```

profile of v0, /device:TPU:1, one launch (start us, length us, event | category | flops | bytes accessed | tf_op | source)
XLA Modules:
  0.0 241.2 jit_solution(15151068722446621680)
XLA Ops:
  0.0 1.6 fusion.12
  1.6 0.1 copy-done
  1.7 3.1 %convolution_convert_fusion.1 = bf16[16,64,1536]{2,1,0:T(8,128)(2,1)S(1)} fusion(bf16[512,1536]{1,0:T(8,128)(2,1)S(1)} %copy-done, bf16[16,64,512]{2,1,0:T(8,128)(2,1)} %param.7, f32[512]{0:T(512)} %param.8, f32[16,64]{1,0:T(8,128)S(1)} %add_rsqrt_fusion.1), kind=kOutput, calls=%fused_computation.15 | convolution fusion | flops 1614282752 | bytes 5773312 | tf_op jit(solution)/shard_map/dot_general | solution.py:36
  4.8 43.0 %all_to_all.72 = bf16[16,64,1536]{2,1,0:T(8,128)(2,1)S(1)} all-to-all(bf16[16,64,1536]{2,1,0:T(8,128)(2,1)S(1)} %convolution_convert_fusion.1), channel_id=1, replica_groups=mesh['rows'=32,'cols'=8] {'cols'}, dimensions={0} | all-to-all | bytes 6291456 | tf_op jit(solution)/shard_map/all_to_all | solution.py:46
  47.8 0.3 copy.42
  48.1 0.3 fusion.39
  48.4 1.3 copy.45
  49.7 1.3 copy.44
  51.0 0.5 copy.43
  51.6 10.0 %fusion.40 = (f32[2,8,512]{2,1,0:T(8,128)S(1)}, f32[2,8,512,512]{2,3,1,0:T(8,128)}) fusion(bf16[2,512,8,64]{1,3,2,0:T(8,128)(2,1)} %bitcast.61, bf16[2,512,8,64]{1,3,2,0:T(8,128)(2,1)S(1)} %bitcast.59), kind=kOutput, calls=%fused_computation.48 | convolution fusion | flops 549454336 | bytes 18907136 | tf_op jit(solution)/shard_map/sub | solution.py:27
  61.5 7.3 %fusion.27 = bf16[2,8,64,512]{3,2,1,0:T(8,128)(2,1)S(1)} fusion(bf16[2,512,8,64]{1,3,2,0:T(8,128)(2,1)S(1)} %bitcast.62, f32[2,8,512,512]{2,3,1,0:T(8,128)} %get-tuple-element.12, f32[2,8,512]{2,1,0:T(8,128)S(1)} %get-tuple-element.11), kind=kOutput, calls=%fused_computation.35 | convolution fusion | flops 545783808 | bytes 18907136 | tf_op jit(solution)/shard_map/lhqk,lkhd->lqhd/dot_general | solution.py:31
  68.9 1.0 copy.47
  69.9 16.2 %all_to_all.73 = bf16[2,512,512]{2,0,1:T(2,128)(2,1)S(1)} all-to-all(bf16[2,512,512]{2,0,1:T(2,128)(2,1)S(1)} %copy.47), channel_id=1, replica_groups=mesh['rows'=32,'cols'=8] {'cols'}, dimensions={1} | all-to-all | bytes 2097152 | tf_op jit(solution)/shard_map/all_to_all | solution.py:50
  86.1 0.2 copy.48
  86.3 0.1 copy.49
  86.4 1.7 fusion.16
  88.1 3.1 %convolution_convert_fusion = bf16[16,64,1536]{2,1,0:T(8,128)(2,1)S(1)} fusion(bf16[512,1536]{1,0:T(8,128)(2,1)S(1)} %copy-done.5, bf16[16,64,512]{2,1,0:T(8,128)(2,1)} %get-tuple-element.14, f32[512]{0:T(512)S(1)} %copy-done.8, f32[16,64]{1,0:T(8,128)S(1)} %add_rsqrt_fusion), kind=kOutput, calls=%fused_computation.14 | convolution fusion | flops 1614282752 | bytes 5773312 | tf_op jit(solution)/shard_map/dot_general | solution.py:36
  91.2 1.7 copy.50
  92.9 86.7 %all_to_all.74 = bf16[16,64,1536]{2,0,1:T(8,128)(2,1)S(1)} all-to-all(bf16[16,64,1536]{2,0,1:T(8,128)(2,1)S(1)} %copy.50), channel_id=1, replica_groups=mesh['rows'=32,'cols'=8] {'rows'}, dimensions={1} | all-to-all | bytes 6291456 | tf_op jit(solution)/shard_map/all_to_all | solution.py:53
  179.6 0.2 copy.51
  179.9 0.3 fusion.38
  180.2 1.3 copy.54
  181.5 1.3 copy.53
  182.8 0.5 copy.52
  183.4 10.0 %fusion.41 = (f32[2,8,512]{2,1,0:T(8,128)S(1)}, f32[2,8,512,512]{2,3,1,0:T(8,128)}) fusion(bf16[512,2,8,64]{0,3,2,1:T(8,128)(2,1)} %bitcast.63, bf16[512,2,8,64]{0,3,2,1:T(8,128)(2,1)S(1)} %bitcast.60), kind=kOutput, calls=%fused_computation.49 | convolution fusion | flops 549454336 | bytes 18907136 | tf_op jit(solution)/shard_map/sub | solution.py:27
  193.4 7.3 %fusion.26 = bf16[2,8,64,512]{3,2,1,0:T(8,128)(2,1)S(1)} fusion(bf16[512,2,8,64]{0,3,2,1:T(8,128)(2,1)S(1)} %bitcast.64, f32[2,8,512,512]{2,3,1,0:T(8,128)} %get-tuple-element.16, f32[2,8,512]{2,1,0:T(8,128)S(1)} %get-tuple-element.15), kind=kOutput, calls=%fused_computation.34 | convolution fusion | flops 545783808 | bytes 18907136 | tf_op jit(solution)/shard_map/lhqk,klhd->qlhd/dot_general | solution.py:29
  200.7 1.0 copy.56
  201.7 33.8 %all_to_all.75 = bf16[512,2,512]{2,1,0:T(2,128)(2,1)S(1)} all-to-all(bf16[512,2,512]{2,1,0:T(2,128)(2,1)S(1)} %copy.56), channel_id=1, replica_groups=mesh['rows'=32,'cols'=8] {'rows'}, dimensions={0} | all-to-all | bytes 2097152 | tf_op jit(solution)/shard_map/all_to_all | solution.py:57
  235.5 0.2 copy.57
  235.6 1.1 copy.58
  236.7 1.2 all_to_all.67
  238.0 3.2 %fusion.19 = bf16[16,64,512]{2,1,0:T(8,128)(2,1)} fusion(bf16[16,64,512]{2,1,0:T(8,128)(2,1)} %get-tuple-element.14, bf16[16,64,512]{2,1,0:T(8,128)(2,1)} %all_to_all.67, bf16[512,512]{1,0:T(8,128)(2,1)S(1)} %copy-done.7), kind=kOutput, calls=%fused_computation.29 | convolution fusion | flops 538443776 | bytes 3670016 | tf_op jit(solution)/shard_map/dot_general | solution.py:40
  (19 shorter events, 0.1 us)
Async XLA Ops:
  0.0 1.7 copy-start
  49.7 1.9 copy-start.3
  69.9 16.5 %copy-start.2 = (bf16[16,64,512]{2,1,0:T(8,128)(2,1)S(1)}, bf16[16,64,512]{2,1,0:T(8,128)(2,1)}, u32[]{:S(2)}) copy-start(bf16[16,64,512]{2,1,0:T(8,128)(2,1)} %param.7) | copy-start | bytes 3145732
  69.9 16.5 %copy-start.6 = (bf16[512,512]{1,0:T(8,128)(2,1)S(1)}, bf16[512,512]{1,0:T(8,128)(2,1)}, u32[]{:S(2)}) copy-start(bf16[512,512]{1,0:T(8,128)(2,1)} %param.10) | copy-start | bytes 1572868
  86.2 1.9 copy-start.5
  86.2 1.9 copy-start.8
  181.5 1.9 copy-start.4
  235.5 2.5 %copy-start.7 = (bf16[512,512]{1,0:T(8,128)(2,1)S(1)}, bf16[512,512]{1,0:T(8,128)(2,1)}, u32[]{:S(2)}) copy-start(bf16[512,512]{1,0:T(8,128)(2,1)} %param.13) | copy-start | bytes 1572868
  235.6 5.6 %copy-start.1 = (bf16[512,1536]{1,0:T(8,128)(2,1)S(1)}, bf16[512,1536]{1,0:T(8,128)(2,1)}, u32[]{:S(2)}) copy-start(bf16[512,1536]{1,0:T(8,128)(2,1)} %param.9) | copy-start | bytes 4718596
where the time goes:
time: 243 us; the launch traced here: 241 us
  blocking collectives  180 us (74%)
  matrix products  45.7 us (19%)
  local copies, waits for them, and re-layouts  14.1 us (6%)
    all_to_all x1, blocking collectives, per_device(): lax.all_to_all(project(normed, qkv_lat), 'rows', split_axis=1, concat_axi...  86.7 us
    all_to_all x1, blocking collectives, per_device(): lax.all_to_all(project(normed, qkv_lon), 'cols', split_axis=0, concat_axi...  43 us
    all_to_all x1, blocking collectives, per_device(): lax.all_to_all(mixed, 'rows', split_axis=0, concat_axis=1, tiled=True)  33.8 us
    sub x2, matrix products, attend(): weights = jax.nn.softmax(scores, axis=-1).astype(jnp.bfloat16)  19.9 us
    all_to_all x1, blocking collectives, per_device(): lax.all_to_all(mixed, 'cols', split_axis=1, concat_axis=0, tiled=True)  16.2 us
    dot_general x1, matrix products, attend(): jnp.einsum('lhqk,lkhd->lqhd', weights, values, preferred_element_type=jnp...  7.34 us
    dot_general x1, matrix products, attend(): jnp.einsum('lhqk,klhd->qlhd', weights, values, preferred_element_type=jnp...  7.34 us
    dot_general x2, matrix products, project(): jnp.dot(normed, w_qkv, preferred_element_type=jnp.float32)  6.17 us

commit v1 on v0

v1 whole, which is shorter than its diff:
```python
import functools

import jax
import jax.numpy as jnp
from jax import lax
from jax.experimental import pallas as pl
from jax.experimental.pallas import tpu as pltpu
from jax.sharding import PartitionSpec as P

D = 512
PAIRS = 4
SEQ = 512
ROWS = 32
COLS = 8
QB = 128
SCALE = 64 ** (-0.5) * 1.4426950408889634
MESH = pl.DeviceIdType.MESH
BF16 = jnp.bfloat16
F32 = jnp.float32


def arrived(ref, sem):
    pltpu.make_async_copy(ref, ref, sem).wait()


def selection(n, source):
    out = lax.broadcasted_iota(jnp.int32, (n, n), 0)
    take = lax.broadcasted_iota(jnp.int32, (n, n), 1)
    return (take == source(out)).astype(F32).astype(BF16)


def norm(x, gain):
    scale = lax.rsqrt(jnp.mean(x * x, axis=-1, keepdims=True) + 1e-06)
    return (x * scale * gain).astype(BF16)


def project(x, gain, w_ref, q_ref, kt_ref, v_ref, line, at, n):
    normed = norm(x.astype(F32), gain)
    q = jnp.dot(normed, w_ref[:, :D], preferred_element_type=F32)
    q_ref[line, pl.ds(at, n), :] = (q * SCALE).astype(BF16)
    k = jnp.dot(normed, w_ref[:, D : 2 * D], preferred_element_type=F32)
    kt_ref[line, :, pl.ds(at, n)] = k.T.astype(BF16)
    v = jnp.dot(normed, w_ref[:, 2 * D :], preferred_element_type=F32)
    low = lax.broadcasted_iota(jnp.int32, (n, 128), 1) < 64
    for p in range(PAIRS):
        vp = v[:, 128 * p : 128 * p + 128]
        v_ref[line, p, pl.ds(at, n), :128] = jnp.where(low, vp, 0.0).astype(BF16)
        v_ref[line, p, pl.ds(SEQ + at, n), :128] = jnp.where(low, 0.0, vp).astype(BF16)


def attend(q_ref, kt_ref, v_ref, line, at):
    low = lax.broadcasted_iota(jnp.int32, (QB, 128), 1) < 64
    mixed = []
    for p in range(PAIRS):
        q = q_ref[line, pl.ds(at, QB), 128 * p : 128 * p + 128].astype(F32)
        both = jnp.concatenate([jnp.where(low, q, 0.0), jnp.where(low, 0.0, q)], axis=0).astype(BF16)
        scores = jnp.dot(both, kt_ref[line, 128 * p : 128 * p + 128, :], preferred_element_type=F32)
        weights = jnp.exp2(scores - jnp.max(scores, axis=-1, keepdims=True)).astype(BF16)
        weights = jnp.concatenate([weights[:QB], weights[QB:]], axis=1)
        total = jnp.dot(weights, v_ref[line, p], preferred_element_type=F32)
        mixed.append((total[:, :128] / total[:, 128:]).astype(BF16))
    return jnp.concatenate(mixed, axis=1)


def kernel(
    grid_ref, gain_lon, qkv_lon, out_lon, gain_lat, qkv_lat, out_lat, result_ref,
    w1, o1, w2, o2, x1, x2, q_ref, kt_ref, v_ref, pick, pick3, away, here, done, back, final,
    w_sem, x_sem, x_sent, h_sem, h_sent, b_sem, b_sent, f_sem,
):
    r, c = lax.axis_index("rows"), lax.axis_index("cols")
    loads = [
        pltpu.make_async_copy(src, dst, w_sem.at[n])
        for n, (src, dst) in enumerate([(qkv_lon, w1), (out_lon, o1), (qkv_lat, w2), (out_lat, o2)])
    ]
    for load in loads:
        load.start()

    barrier = pltpu.get_barrier_semaphore()

    @pl.loop(1, COLS)
    def _(k):
        pl.semaphore_signal(barrier, inc=1, device_id=(r, lax.rem(c + k, COLS)), device_id_type=MESH)

    @pl.loop(1, ROWS)
    def _(k):
        pl.semaphore_signal(barrier, inc=1, device_id=(lax.rem(r + k, ROWS), c), device_id_type=MESH)

    pick[0] = selection(128, lambda o: (o % 16 // 2) * 16 + 2 * (o // 16) + o % 2)
    pick[1] = selection(128, lambda o: (o % 16 // 2) * 16 + (o // 32) * 4 + (o % 2) * 2 + o // 16 % 2)
    pick3[...] = selection(256, lambda o: (o % 16) * 16 + o // 16)
    ones = (lax.broadcasted_iota(jnp.int32, (SEQ, 128), 1) < 64).astype(F32)
    for line in range(2):
        for p in range(PAIRS):
            v_ref[line, p, :SEQ, 128:] = ones.astype(BF16)
            v_ref[line, p, SEQ:, 128:] = (1.0 - ones).astype(BF16)

    pl.semaphore_wait(barrier, ROWS + COLS - 2)

    for i in range(2):
        pltpu.make_async_copy(grid_ref.at[2 * c + i], x1.at[i, pl.ds(64 * c, 64)], x_sem.at[i]).start()

        @pl.loop(1, COLS)
        def _(k):
            to = lax.rem(c + k, COLS)
            pltpu.make_async_remote_copy(
                grid_ref.at[2 * to + i], x1.at[i, pl.ds(64 * c, 64)], x_sent.at[i], x_sem.at[i],
                device_id=(r, to), device_id_type=MESH,
            ).start()

    loads[0].wait()
    for i in range(2):
        arrived(x1.at[i], x_sem.at[i])
        project(x1[i], gain_lon[...], w1, q_ref, kt_ref, v_ref, i, 0, SEQ)
    loads[1].wait()

    @pl.loop(0, SEQ // QB)
    def _(step):
        block = lax.rem(step + c // 2, SEQ // QB)
        at = pl.multiple_of(block * QB, QB)
        first = []
        for i in range(2):
            mixed = attend(q_ref, kt_ref, v_ref, i, at)
            total = x1[i, pl.ds(at, QB), :].astype(F32) + jnp.dot(mixed, o1[...], preferred_element_type=F32)
            first.append(total.astype(BF16))
        for g in range(QB // 16):
            cells = jnp.concatenate(
                [first[i][16 * g : 16 * g + 16, 128 * f : 128 * f + 128] for f in range(4) for i in range(2)], axis=0
            )
            cells = jnp.dot(pick[0], cells, preferred_element_type=F32).astype(BF16)
            away[pl.ds(block * (QB // 2) + 8 * g, 8)] = cells.reshape(8, 16, 128)

        @pl.loop(0, ROWS)
        def _(k):
            to_r = lax.rem(r + k, ROWS)
            for n in range(2):
                to_c = 2 * block + n
                own = jnp.logical_and(k == 0, to_c == c)
                src, dst = away.at[to_c * ROWS + to_r], here.at[r * COLS + c]

                @pl.when(own)
                def _():
                    pltpu.make_async_copy(src, dst, h_sem).start()

                @pl.when(jnp.logical_not(own))
                def _():
                    pltpu.make_async_remote_copy(
                        src, dst, h_sent, h_sem, device_id=(to_r, to_c), device_id_type=MESH
                    ).start()

    for load in loads[2:]:
        load.wait()
    arrived(here, h_sem)

    @pl.loop(0, ROWS // 2)
    def _(n):
        pair = [here[pl.ds((2 * n + m) * COLS, COLS)].reshape(128, 128) for m in range(2)]
        cells = jnp.dot(pick[1], jnp.concatenate(pair, axis=1), preferred_element_type=F32).astype(BF16)
        for m in range(2):
            for f in range(4):
                for j in range(2):
                    x2[j, pl.ds((2 * n + m) * 16, 16), 128 * f : 128 * f + 128] = cells[
                        32 * f + 16 * j : 32 * f + 16 * j + 16, 128 * m : 128 * m + 128
                    ]

    for j in range(2):
        project(x2[j], gain_lat[...], w2, q_ref, kt_ref, v_ref, j, 0, SEQ)

        @pl.loop(0, SEQ // QB)
        def _(step):
            block = lax.rem(step + r // 8, SEQ // QB)
            at = pl.multiple_of(block * QB, QB)
            mixed = attend(q_ref, kt_ref, v_ref, j, at)
            total = x2[j, pl.ds(at, QB), :].astype(F32) + jnp.dot(mixed, o2[...], preferred_element_type=F32)
            done[j, pl.ds(at, QB), :] = total.astype(BF16)

            @pl.loop(0, QB // 16)
            def _(k):
                to = block * (QB // 16) + lax.rem(r + k, QB // 16)
                src = done.at[j, pl.ds(pl.multiple_of(to * 16, 16), 16)]
                dst = back.at[2 * r + j]

                @pl.when(to == r)
                def _():
                    pltpu.make_async_copy(src, dst, b_sem.at[r // 8]).start()

                @pl.when(to != r)
                def _():
                    pltpu.make_async_remote_copy(
                        src, dst, b_sent, b_sem.at[r // 8], device_id=(to, c), device_id_type=MESH
                    ).start()

    for g in range(4):
        arrived(back.at[pl.ds(16 * g, 16)], b_sem.at[g])
        cells = back[pl.ds(16 * g, 16)].reshape(256, D)
        cells = jnp.dot(pick3[...], cells, preferred_element_type=F32).astype(BF16)
        final[:, 16 * g : 16 * g + 16, :] = cells.reshape(16, 16, D)
    pltpu.make_async_copy(final, result_ref, f_sem).start()

    for i in range(2):
        arrived(x1.at[i, pl.ds(0, 64 * (COLS - 1))], x_sent.at[i])
    arrived(away.at[pl.ds(0, ROWS * COLS - 1)], h_sent)
    arrived(back.at[pl.ds(0, 2 * (ROWS - 1))], b_sent)
    pltpu.make_async_copy(final, result_ref, f_sem).wait()


def per_device(grid, gain_lon, qkv_lon, out_lon, gain_lat, qkv_lat, out_lat):
    place = pl.BlockSpec(memory_space=pl.ANY)
    whole = pl.BlockSpec(memory_space=pltpu.VMEM)
    dma = pltpu.SemaphoreType.DMA
    return pl.pallas_call(
        kernel,
        out_shape=jax.ShapeDtypeStruct((16, 64, D), BF16),
        in_specs=[place, whole, place, place, whole, place, place],
        out_specs=place,
        scratch_shapes=[
            pltpu.VMEM((D, 3 * D), BF16),
            pltpu.VMEM((D, D), BF16),
            pltpu.VMEM((D, 3 * D), BF16),
            pltpu.VMEM((D, D), BF16),
            pltpu.VMEM((2, SEQ, D), BF16),
            pltpu.VMEM((2, SEQ, D), BF16),
            pltpu.VMEM((2, SEQ, D), BF16),
            pltpu.VMEM((2, D, SEQ), BF16),
            pltpu.VMEM((2, PAIRS, 2 * SEQ, 256), BF16),
            pltpu.VMEM((2, 128, 128), BF16),
            pltpu.VMEM((256, 256), BF16),
            pltpu.VMEM((ROWS * COLS, 16, 128), BF16),
            pltpu.VMEM((ROWS * COLS, 16, 128), BF16),
            pltpu.VMEM((2, SEQ, D), BF16),
            pltpu.VMEM((64, 16, D), BF16),
            pltpu.VMEM((16, 64, D), BF16),
            dma((4,)),
            dma((2,)),
            dma((2,)),
            dma,
            dma,
            dma((4,)),
            dma,
            dma,
        ],
        compiler_params=pltpu.CompilerParams(
            collective_id=0, has_side_effects=True, vmem_limit_bytes=48 * 2**20
        ),
        cost_estimate=pl.CostEstimate(flops=6 * 10**9, bytes_accessed=8 * 2**20, transcendentals=8 * 2**20),
    )(grid, gain_lon.reshape(1, D), qkv_lon, out_lon, gain_lat.reshape(1, D), qkv_lat, out_lat)


def solution(mesh):
    return jax.shard_map(
        per_device,
        mesh=mesh,
        in_specs=(P("rows", "cols", None), P(), P(), P(), P(), P(), P()),
        out_specs=P("rows", "cols", None),
        check_vma=False,
    )
```

time: 243 us -> 94.2 us (0.39)
  blocking collectives: 180 us -> 0 us
  Pallas kernels: 0 us -> 86.9 us
  matrix products: 45.7 us -> 0 us
  local copies, waits for them, and re-layouts: 14.1 us -> 7.05 us
    all_to_all x4 -> x0, blocking collectives: 180 us -> none  [the longest x1 86.7 us: per_device(): lax.all_to_all(project(normed, qkv_lat), 'rows', split_axis=1, concat_axi...]
    pallas_call x0 -> x1, Pallas kernels: none -> 86.9 us  [per_device(): pl.pallas_call(kernel, out_shape=jax.ShapeDtypeStruct((16, 64, D), BF16),...]
    dot_general x6 -> x0, matrix products: 25.8 us -> none  [the longest x1 7.34 us: attend(): jnp.einsum('lhqk,lkhd->lqhd', weights, values, preferred_element_type=jnp...]
    sub x2 -> x0, matrix products: 19.9 us -> none  [attend(): weights = jax.nn.softmax(scores, axis=-1).astype(jnp.bfloat16)]
    slice x8 -> x0, local copies, waits for them, and re-layouts: 6.99 us -> none  [the longest x4 3.27 us: attend(): keys = proj[..., width:2 * width].reshape(lead + (HEADS, head_size))]
    unnamed x18 -> x13, local copies, waits for them, and re-layouts: 0.13 us -> 7.05 us
    all_to_all x7 -> x0, local copies, waits for them, and re-layouts: 3.24 us -> none  [the longest x3 2.48 us: per_device(): lax.all_to_all(mixed, 'rows', split_axis=0, concat_axis=1, tiled=True)]
where the time goes in v1:
time: 94.2 us; the launch traced here: 94 us
  Pallas kernels  86.9 us (92%)
  local copies, waits for them, and re-layouts  7.05 us (7%)
    pallas_call x1, Pallas kernels, per_device(): pl.pallas_call(kernel, out_shape=jax.ShapeDtypeStruct((16, 64, D), BF16),...  86.9 us
    unnamed x13, local copies, waits for them, and re-layouts  7.05 us

profile of v1, /device:TPU:1, one launch (start us, length us, event | category | flops | bytes accessed | tf_op | source)
XLA Modules:
  0.0 94.0 jit_solution(77490343864840085)
XLA Ops:
  0.0 0.0 copy-start
  0.0 1.4 %copy-done = bf16[512,1536]{1,0:T(8,128)(2,1)S(1)} copy-done((bf16[512,1536]{1,0:T(8,128)(2,1)S(1)}, bf16[512,1536]{1,0:T(8,128)(2,1)}, u32[]{:S(2)}) %copy-start) | copy-done | bytes 1572888
  1.4 0.0 copy-start.1
  1.4 1.2 %copy-done.1 = bf16[16,64,512]{2,1,0:T(8,128)(2,1)S(1)} copy-done((bf16[16,64,512]{2,1,0:T(8,128)(2,1)S(1)}, bf16[16,64,512]{2,1,0:T(8,128)(2,1)}, u32[]{:S(2)}) %copy-start.1) | copy-done | bytes 1048600
  2.6 0.0 copy-start.2
  2.6 1.0 %copy-done.2 = bf16[512,512]{1,0:T(8,128)(2,1)S(1)} copy-done((bf16[512,512]{1,0:T(8,128)(2,1)S(1)}, bf16[512,512]{1,0:T(8,128)(2,1)}, u32[]{:S(2)}) %copy-start.2) | copy-done | bytes 524312
  3.7 0.0 copy-start.3
  3.7 1.0 %copy-done.3 = bf16[512,512]{1,0:T(8,128)(2,1)S(1)} copy-done((bf16[512,512]{1,0:T(8,128)(2,1)S(1)}, bf16[512,512]{1,0:T(8,128)(2,1)}, u32[]{:S(2)}) %copy-start.3) | copy-done | bytes 524312
  4.7 0.0 copy-start.4
  4.7 0.7 copy-done.4
  5.4 0.0 copy-start.5
  5.4 0.7 copy-done.5
  6.1 86.9 %shard_map.73 = bf16[16,64,512]{2,1,0:T(8,128)(2,1)S(1)} custom-call(bf16[16,64,512]{2,1,0:T(8,128)(2,1)S(1)} %copy-done.1, f32[1,512]{1,0:T(1,128)S(1)} %bitcast.2, bf16[512,1536]{1,0:T(8,128)(2,1)S(1)} %copy-done, bf16[512,512]{1,0:T(8,128)(2,1)S(1)} %copy-done.2, f32[1,512]{1,0:T(1,128)S(1)} %bitcast.3, bf16[512,1536]{1,0:T(8,128)(2,1)} %qkv_lat.1, ...), custom_call_target="tpu_custom_call" | custom-call | flops 6000000000 | bytes 8388608 | tf_op jit(solution)/shard_map/pallas_call | solution.py:210
  93.0 1.0 %copy.9 = bf16[16,64,512]{2,1,0:T(8,128)(2,1)} copy(bf16[16,64,512]{2,1,0:T(8,128)(2,1)S(1)} %shard_map.73) | data formatting | bytes 2097152
Async XLA Ops:
  0.0 1.4 %copy-start = (bf16[512,1536]{1,0:T(8,128)(2,1)S(1)}, bf16[512,1536]{1,0:T(8,128)(2,1)}, u32[]{:S(2)}) copy-start(bf16[512,1536]{1,0:T(8,128)(2,1)} %qkv_lon.1) | copy-start | bytes 4718596
  1.4 1.2 %copy-start.1 = (bf16[16,64,512]{2,1,0:T(8,128)(2,1)S(1)}, bf16[16,64,512]{2,1,0:T(8,128)(2,1)}, u32[]{:S(2)}) copy-start(bf16[16,64,512]{2,1,0:T(8,128)(2,1)} %grid_ref.1) | copy-start | bytes 3145732
  2.6 1.0 %copy-start.2 = (bf16[512,512]{1,0:T(8,128)(2,1)S(1)}, bf16[512,512]{1,0:T(8,128)(2,1)}, u32[]{:S(2)}) copy-start(bf16[512,512]{1,0:T(8,128)(2,1)} %out_lon.1) | copy-start | bytes 1572868
  3.7 1.0 %copy-start.3 = (bf16[512,512]{1,0:T(8,128)(2,1)S(1)}, bf16[512,512]{1,0:T(8,128)(2,1)}, u32[]{:S(2)}) copy-start(bf16[512,512]{1,0:T(8,128)(2,1)} %out_lat.1) | copy-start | bytes 1572868
  4.7 0.7 copy-start.4
  5.4 0.7 copy-start.5

commit v2 on v1

--- a/solution.py
+++ b/solution.py
@@ -65,9 +65,11 @@
 def kernel(
     grid_ref, gain_lon, qkv_lon, out_lon, gain_lat, qkv_lat, out_lat, result_ref,
     w1, o1, w2, o2, x1, x2, q_ref, kt_ref, v_ref, pick, pick3, away, here, done, back, final,
-    w_sem, x_sem, x_sent, h_sem, h_sent, b_sem, b_sent, f_sem,
+    w_sem, x_sem, x_sent, go, h_sem, h_sent, b_sem, b_sent, f_sem,
 ):
     r, c = lax.axis_index("rows"), lax.axis_index("cols")
+    core, chip = lax.rem(r, 2), r // 2
+    place = core * 16 + chip
     loads = [
         pltpu.make_async_copy(src, dst, w_sem.at[n])
         for n, (src, dst) in enumerate([(qkv_lon, w1), (out_lon, o1), (qkv_lat, w2), (out_lat, o2)])
@@ -97,30 +99,44 @@
     pl.semaphore_wait(barrier, ROWS + COLS - 2)
 
     for i in range(2):
-        pltpu.make_async_copy(grid_ref.at[2 * c + i], x1.at[i, pl.ds(64 * c, 64)], x_sem.at[i]).start()
+        pltpu.make_async_copy(grid_ref.at[2 * c + i], x1.at[i, :, c], x_sem.at[i]).start()
+
+    @pl.when(core == 1)
+    def _():
+        pl.semaphore_wait(go, 1)
+
+    for i in range(2):
 
         @pl.loop(1, COLS)
         def _(k):
             to = lax.rem(c + k, COLS)
             pltpu.make_async_remote_copy(
-                grid_ref.at[2 * to + i], x1.at[i, pl.ds(64 * c, 64)], x_sent.at[i], x_sem.at[i],
+                grid_ref.at[2 * to + i], x1.at[i, :, c], x_sent.at[i], x_sem.at[i],
                 device_id=(r, to), device_id_type=MESH,
             ).start()
 
     loads[0].wait()
     for i in range(2):
         arrived(x1.at[i], x_sem.at[i])
-        project(x1[i], gain_lon[...], w1, q_ref, kt_ref, v_ref, i, 0, SEQ)
+        if i == 0:
+
+            @pl.when(core == 0)
+            def _():
+                pl.semaphore_signal(go, inc=1, device_id=(r + 1, c), device_id_type=MESH)
+
+        project(x1[i].reshape(SEQ, D), gain_lon[...], w1, q_ref, kt_ref, v_ref, i, 0, SEQ)
     loads[1].wait()
 
     @pl.loop(0, SEQ // QB)
     def _(step):
-        block = lax.rem(step + c // 2, SEQ // QB)
+        to_core, part = step // 2, lax.rem(step + chip, 2)
+        block = 2 * to_core + part
         at = pl.multiple_of(block * QB, QB)
         first = []
         for i in range(2):
             mixed = attend(q_ref, kt_ref, v_ref, i, at)
-            total = x1[i, pl.ds(at, QB), :].astype(F32) + jnp.dot(mixed, o1[...], preferred_element_type=F32)
+            base = x1[i, to_core, pl.ds(4 * part, 4)].reshape(QB, D)
+            total = base.astype(F32) + jnp.dot(mixed, o1[...], preferred_element_type=F32)
             first.append(total.astype(BF16))
         for g in range(QB // 16):
             cells = jnp.concatenate(
@@ -129,78 +145,106 @@
             cells = jnp.dot(pick[0], cells, preferred_element_type=F32).astype(BF16)
             away[pl.ds(block * (QB // 2) + 8 * g, 8)] = cells.reshape(8, 16, 128)
 
-        @pl.loop(0, ROWS)
+        def send(k, n):
+            to_chip = lax.rem(chip + k, ROWS // 2)
+            turn = lax.rem(c + n, 4)
+            to = (2 * to_chip + to_core, 4 * part + turn)
+            src, dst = away.at[64 * block + 16 * turn + to_chip], here.at[COLS * place + c]
+            return to, src, dst, pltpu.make_async_remote_copy(
+                src, dst, h_sent, h_sem.at[core], device_id=to, device_id_type=MESH
+            )
+
+        for n in range(4):
+            to, src, dst, copy = send(0, n)
+            own = jnp.logical_and(to[0] == r, to[1] == c)
+
+            @pl.when(own)
+            def _():
+                pltpu.make_async_copy(src, dst, h_sem.at[core]).start()
+
+            @pl.when(jnp.logical_not(own))
+            def _():
+                copy.start()
+
+        @pl.loop(1, ROWS // 2)
         def _(k):
-            to_r = lax.rem(r + k, ROWS)
-            for n in range(2):
-                to_c = 2 * block + n
-                own = jnp.logical_and(k == 0, to_c == c)
-                src, dst = away.at[to_c * ROWS + to_r], here.at[r * COLS + c]
-
-                @pl.when(own)
-                def _():
-                    pltpu.make_async_copy(src, dst, h_sem).start()
-
-                @pl.when(jnp.logical_not(own))
-                def _():
-                    pltpu.make_async_remote_copy(
-                        src, dst, h_sent, h_sem, device_id=(to_r, to_c), device_id_type=MESH
-                    ).start()
+            for n in range(4):
+                send(k, n)[-1].start()
 
     for load in loads[2:]:
         load.wait()
-    arrived(here, h_sem)
-
-    @pl.loop(0, ROWS // 2)
-    def _(n):
-        pair = [here[pl.ds((2 * n + m) * COLS, COLS)].reshape(128, 128) for m in range(2)]
-        cells = jnp.dot(pick[1], jnp.concatenate(pair, axis=1), preferred_element_type=F32).astype(BF16)
-        for m in range(2):
-            for f in range(4):
-                for j in range(2):
-                    x2[j, pl.ds((2 * n + m) * 16, 16), 128 * f : 128 * f + 128] = cells[
-                        32 * f + 16 * j : 32 * f + 16 * j + 16, 128 * m : 128 * m + 128
-                    ]
+
+    half = ROWS * COLS // 2
+    for h in range(2):
+        arrived(here.at[pl.ds(half * h, half)], h_sem.at[h])
+
+        @pl.loop(0, ROWS // 4)
+        def _(n):
+            first = ROWS // 2 * h + 2 * n
+            pair = [here[pl.ds((first + m) * COLS, COLS)].reshape(128, 128) for m in range(2)]
+            cells = jnp.dot(pick[1], jnp.concatenate(pair, axis=1), preferred_element_type=F32).astype(BF16)
+            for m in range(2):
+                for f in range(4):
+                    for j in range(2):
+                        x2[j, pl.ds((first + m) * 16, 16), 128 * f : 128 * f + 128] = cells[
+                            32 * f + 16 * j : 32 * f + 16 * j + 16, 128 * m : 128 * m + 128
+                        ]
+
+        for j in range(2):
+            n = SEQ // 2
+            project(x2[j, n * h : n * h + n], gain_lat[...], w2, q_ref, kt_ref, v_ref, j, n * h, n)
 
     for j in range(2):
-        project(x2[j], gain_lat[...], w2, q_ref, kt_ref, v_ref, j, 0, SEQ)
 
         @pl.loop(0, SEQ // QB)
         def _(step):
-            block = lax.rem(step + r // 8, SEQ // QB)
+            block = lax.rem(step + place // 8, SEQ // QB)
             at = pl.multiple_of(block * QB, QB)
             mixed = attend(q_ref, kt_ref, v_ref, j, at)
             total = x2[j, pl.ds(at, QB), :].astype(F32) + jnp.dot(mixed, o2[...], preferred_element_type=F32)
             done[j, pl.ds(at, QB), :] = total.astype(BF16)
 
-            @pl.loop(0, QB // 16)
+            def send(k):
+                to_place = 8 * block + lax.rem(place + k, 8)
+                to = 2 * lax.rem(to_place, 16) + to_place // 16
+                src, dst = done.at[j, pl.ds(pl.multiple_of(16 * to_place, 16), 16)], back.at[2 * place + j]
+                return to, src, dst, pltpu.make_async_remote_copy(
+                    src, dst, b_sent, b_sem.at[place // 8], device_id=(to, c), device_id_type=MESH
+                )
+
+            to, src, dst, copy = send(0)
+
+            @pl.when(to == r)
+            def _():
+                pltpu.make_async_copy(src, dst, b_sem.at[place // 8]).start()
+
+            @pl.when(to != r)
+            def _():
+                copy.start()
+
+            @pl.loop(1, QB // 16)
             def _(k):
-                to = block * (QB // 16) + lax.rem(r + k, QB // 16)
-                src = done.at[j, pl.ds(pl.multiple_of(to * 16, 16), 16)]
-                dst = back.at[2 * r + j]
-
-                @pl.when(to == r)
-                def _():
-                    pltpu.make_async_copy(src, dst, b_sem.at[r // 8]).start()
-
-                @pl.when(to != r)
-                def _():
-                    pltpu.make_async_remote_copy(
-                        src, dst, b_sent, b_sem.at[r // 8], device_id=(to, c), device_id_type=MESH
-                    ).start()
-
+                send(k)[-1].start()
+
+    outs = []
     for g in range(4):
         arrived(back.at[pl.ds(16 * g, 16)], b_sem.at[g])
         cells = back[pl.ds(16 * g, 16)].reshape(256, D)
         cells = jnp.dot(pick3[...], cells, preferred_element_type=F32).astype(BF16)
         final[:, 16 * g : 16 * g + 16, :] = cells.reshape(16, 16, D)
-    pltpu.make_async_copy(final, result_ref, f_sem).start()
+        outs.append(
+            pltpu.make_async_copy(
+                final.at[:, pl.ds(16 * g, 16)], result_ref.at[:, pl.ds(16 * g, 16)], f_sem.at[g]
+            )
+        )
+        outs[-1].start()
 
     for i in range(2):
-        arrived(x1.at[i, pl.ds(0, 64 * (COLS - 1))], x_sent.at[i])
+        arrived(x1.at[i, :, pl.ds(0, COLS - 1)], x_sent.at[i])
     arrived(away.at[pl.ds(0, ROWS * COLS - 1)], h_sent)
     arrived(back.at[pl.ds(0, 2 * (ROWS - 1))], b_sent)
-    pltpu.make_async_copy(final, result_ref, f_sem).wait()
+    for out in outs:
+        out.wait()
 
 
 def per_device(grid, gain_lon, qkv_lon, out_lon, gain_lat, qkv_lat, out_lat):
@@ -217,7 +261,7 @@
             pltpu.VMEM((D, D), BF16),
             pltpu.VMEM((D, 3 * D), BF16),
             pltpu.VMEM((D, D), BF16),
-            pltpu.VMEM((2, SEQ, D), BF16),
+            pltpu.VMEM((2, 2, COLS, 32, D), BF16),
             pltpu.VMEM((2, SEQ, D), BF16),
             pltpu.VMEM((2, SEQ, D), BF16),
             pltpu.VMEM((2, D, SEQ), BF16),
@@ -232,17 +276,18 @@
             dma((4,)),
             dma((2,)),
             dma((2,)),
-            dma,
+            pltpu.SemaphoreType.REGULAR,
+            dma((2,)),
             dma,
             dma((4,)),
             dma,
-            dma,
+            dma((4,)),
         ],
         compiler_params=pltpu.CompilerParams(
             collective_id=0, has_side_effects=True, vmem_limit_bytes=48 * 2**20
         ),
         cost_estimate=pl.CostEstimate(flops=6 * 10**9, bytes_accessed=8 * 2**20, transcendentals=8 * 2**20),
-    )(grid, gain_lon.reshape(1, D), qkv_lon, out_lon, gain_lat.reshape(1, D), qkv_lat, out_lat)
+    )(grid.reshape(16, 2, 32, D), gain_lon.reshape(1, D), qkv_lon, out_lon, gain_lat.reshape(1, D), qkv_lat, out_lat)
 
 
 def solution(mesh):

time: 94.2 us -> 86.2 us (0.915)
  Pallas kernels: 86.9 us -> 78.8 us
    pallas_call x1, Pallas kernels: 86.9 us -> 78.8 us  [per_device(): pl.pallas_call(kernel, out_shape=jax.ShapeDtypeStruct((16, 64, D), BF16),...]
where the time goes in v2:
time: 86.2 us; the launch traced here: 85.9 us
  Pallas kernels  78.8 us (91%)
  local copies, waits for them, and re-layouts  7.05 us (8%)
    pallas_call x1, Pallas kernels, per_device(): pl.pallas_call(kernel, out_shape=jax.ShapeDtypeStruct((16, 64, D), BF16),...  78.8 us
    unnamed x13, local copies, waits for them, and re-layouts  7.05 us

profile of v2, /device:TPU:1, one launch (start us, length us, event | category | flops | bytes accessed | tf_op | source)
XLA Modules:
  0.0 85.9 jit_solution(17998627689530613415)
XLA Ops:
  0.0 0.0 copy-start
  0.0 1.4 %copy-done = bf16[512,1536]{1,0:T(8,128)(2,1)S(1)} copy-done((bf16[512,1536]{1,0:T(8,128)(2,1)S(1)}, bf16[512,1536]{1,0:T(8,128)(2,1)}, u32[]{:S(2)}) %copy-start) | copy-done | bytes 1572888
  1.4 0.0 copy-start.1
  1.4 1.2 %copy-done.1 = bf16[16,64,512]{2,1,0:T(8,128)(2,1)S(1)} copy-done((bf16[16,64,512]{2,1,0:T(8,128)(2,1)S(1)}, bf16[16,64,512]{2,1,0:T(8,128)(2,1)}, u32[]{:S(2)}) %copy-start.1) | copy-done | bytes 1048600
  2.6 0.0 copy-start.2
  2.6 1.0 %copy-done.2 = bf16[512,512]{1,0:T(8,128)(2,1)S(1)} copy-done((bf16[512,512]{1,0:T(8,128)(2,1)S(1)}, bf16[512,512]{1,0:T(8,128)(2,1)}, u32[]{:S(2)}) %copy-start.2) | copy-done | bytes 524312
  3.7 0.0 copy-start.3
  3.7 1.0 %copy-done.3 = bf16[512,512]{1,0:T(8,128)(2,1)S(1)} copy-done((bf16[512,512]{1,0:T(8,128)(2,1)S(1)}, bf16[512,512]{1,0:T(8,128)(2,1)}, u32[]{:S(2)}) %copy-start.3) | copy-done | bytes 524312
  4.7 0.0 copy-start.4
  4.7 0.7 copy-done.4
  5.4 0.0 copy-start.5
  5.4 0.7 copy-done.5
  6.1 78.8 %shard_map.73 = bf16[16,64,512]{2,1,0:T(8,128)(2,1)S(1)} custom-call(bf16[16,2,32,512]{3,2,1,0:T(8,128)(2,1)S(1)} %bitcast.3, f32[1,512]{1,0:T(1,128)S(1)} %bitcast.4, bf16[512,1536]{1,0:T(8,128)(2,1)S(1)} %copy-done, bf16[512,512]{1,0:T(8,128)(2,1)S(1)} %copy-done.2, f32[1,512]{1,0:T(1,128)S(1)} %bitcast.5, bf16[512,1536]{1,0:T(8,128)(2,1)} %qkv_lat.1, ...), custom_call_target="tpu_custom_call" | custom-call | flops 6000000000 | bytes 8388608 | tf_op jit(solution)/shard_map/pallas_call | solution.py:254
  84.9 1.0 %copy.9 = bf16[16,64,512]{2,1,0:T(8,128)(2,1)} copy(bf16[16,64,512]{2,1,0:T(8,128)(2,1)S(1)} %shard_map.73) | data formatting | bytes 2097152
Async XLA Ops:
  0.0 1.4 %copy-start = (bf16[512,1536]{1,0:T(8,128)(2,1)S(1)}, bf16[512,1536]{1,0:T(8,128)(2,1)}, u32[]{:S(2)}) copy-start(bf16[512,1536]{1,0:T(8,128)(2,1)} %qkv_lon.1) | copy-start | bytes 4718596
  1.4 1.2 %copy-start.1 = (bf16[16,64,512]{2,1,0:T(8,128)(2,1)S(1)}, bf16[16,64,512]{2,1,0:T(8,128)(2,1)}, u32[]{:S(2)}) copy-start(bf16[16,64,512]{2,1,0:T(8,128)(2,1)} %param.7) | copy-start | bytes 3145732
  2.6 1.0 %copy-start.2 = (bf16[512,512]{1,0:T(8,128)(2,1)S(1)}, bf16[512,512]{1,0:T(8,128)(2,1)}, u32[]{:S(2)}) copy-start(bf16[512,512]{1,0:T(8,128)(2,1)} %out_lon.1) | copy-start | bytes 1572868
  3.7 1.0 %copy-start.3 = (bf16[512,512]{1,0:T(8,128)(2,1)S(1)}, bf16[512,512]{1,0:T(8,128)(2,1)}, u32[]{:S(2)}) copy-start(bf16[512,512]{1,0:T(8,128)(2,1)} %out_lat.1) | copy-start | bytes 1572868
  4.7 0.7 copy-start.4
  5.4 0.7 copy-start.5

commit v3 on v2

--- a/solution.py
+++ b/solution.py
@@ -64,15 +64,17 @@
 
 def kernel(
     grid_ref, gain_lon, qkv_lon, out_lon, gain_lat, qkv_lat, out_lat, result_ref,
-    w1, o1, w2, o2, x1, x2, q_ref, kt_ref, v_ref, pick, pick3, away, here, done, back, final,
-    w_sem, x_sem, x_sent, go, h_sem, h_sent, b_sem, b_sent, f_sem,
+    g1, w1, o1, g2, w2, o2, x1, x2, q_ref, kt_ref, v_ref, pick, pick3, away, here, done, back, final,
+    w_sem, x_sem, x_sent, go, met, known, h_sem, h_sent, b_sem, b_sent, f_sem,
 ):
     r, c = lax.axis_index("rows"), lax.axis_index("cols")
     core, chip = lax.rem(r, 2), r // 2
     place = core * 16 + chip
     loads = [
         pltpu.make_async_copy(src, dst, w_sem.at[n])
-        for n, (src, dst) in enumerate([(qkv_lon, w1), (out_lon, o1), (qkv_lat, w2), (out_lat, o2)])
+        for n, (src, dst) in enumerate(
+            [(gain_lon, g1), (qkv_lon, w1), (out_lon, o1), (gain_lat, g2), (qkv_lat, w2), (out_lat, o2)]
+        )
     ]
     for load in loads:
         load.start()
@@ -83,12 +85,18 @@
     def _(k):
         pl.semaphore_signal(barrier, inc=1, device_id=(r, lax.rem(c + k, COLS)), device_id_type=MESH)
 
-    @pl.loop(1, ROWS)
+    four = [r + (1 - 2 * core), lax.rem(r + 16, ROWS), lax.rem(r + 16, ROWS) + (1 - 2 * core)]
+
+    @pl.loop(1, 8)
     def _(k):
-        pl.semaphore_signal(barrier, inc=1, device_id=(lax.rem(r + k, ROWS), c), device_id_type=MESH)
-
-    pick[0] = selection(128, lambda o: (o % 16 // 2) * 16 + 2 * (o // 16) + o % 2)
-    pick[1] = selection(128, lambda o: (o % 16 // 2) * 16 + (o // 32) * 4 + (o % 2) * 2 + o // 16 % 2)
+        to = r // 16 * 16 + lax.rem(r + 2 * k, 16)
+        pl.semaphore_signal(barrier, inc=1, device_id=(to, c), device_id_type=MESH)
+
+    for to in four:
+        pl.semaphore_signal(barrier, inc=1, device_id=(to, c), device_id_type=MESH)
+
+    pick[0] = selection(128, lambda o: (o % 8 // 2) * 32 + 2 * (o // 8) + o % 2)
+    pick[1] = selection(128, lambda o: (o % 2) * 64 + (o % 16 // 2) * 8 + (o // 32) * 2 + o // 16 % 2)
     pick3[...] = selection(256, lambda o: (o % 16) * 16 + o // 16)
     ones = (lax.broadcasted_iota(jnp.int32, (SEQ, 128), 1) < 64).astype(F32)
     for line in range(2):
@@ -96,7 +104,9 @@
             v_ref[line, p, :SEQ, 128:] = ones.astype(BF16)
             v_ref[line, p, SEQ:, 128:] = (1.0 - ones).astype(BF16)
 
-    pl.semaphore_wait(barrier, ROWS + COLS - 2)
+    pl.semaphore_wait(barrier, 17)
+    for to in four:
+        pl.semaphore_signal(met, inc=1, device_id=(to, c), device_id_type=MESH)
 
     for i in range(2):
         pltpu.make_async_copy(grid_ref.at[2 * c + i], x1.at[i, :, c], x_sem.at[i]).start()
@@ -115,41 +125,25 @@
                 device_id=(r, to), device_id_type=MESH,
             ).start()
 
-    loads[0].wait()
-    for i in range(2):
-        arrived(x1.at[i], x_sem.at[i])
-        if i == 0:
-
-            @pl.when(core == 0)
-            def _():
-                pl.semaphore_signal(go, inc=1, device_id=(r + 1, c), device_id_type=MESH)
-
-        project(x1[i].reshape(SEQ, D), gain_lon[...], w1, q_ref, kt_ref, v_ref, i, 0, SEQ)
-    loads[1].wait()
-
-    @pl.loop(0, SEQ // QB)
-    def _(step):
-        to_core, part = step // 2, lax.rem(step + chip, 2)
+    def row_block(i, to_core, part):
         block = 2 * to_core + part
         at = pl.multiple_of(block * QB, QB)
-        first = []
-        for i in range(2):
-            mixed = attend(q_ref, kt_ref, v_ref, i, at)
-            base = x1[i, to_core, pl.ds(4 * part, 4)].reshape(QB, D)
-            total = base.astype(F32) + jnp.dot(mixed, o1[...], preferred_element_type=F32)
-            first.append(total.astype(BF16))
-        for g in range(QB // 16):
+        mixed = attend(q_ref, kt_ref, v_ref, i, at)
+        base = x1[i, to_core, pl.ds(4 * part, 4)].reshape(QB, D)
+        first = base.astype(F32) + jnp.dot(mixed, o1[...], preferred_element_type=F32)
+        first = first.astype(BF16)
+        for g in range(QB // 32):
             cells = jnp.concatenate(
-                [first[i][16 * g : 16 * g + 16, 128 * f : 128 * f + 128] for f in range(4) for i in range(2)], axis=0
+                [first[32 * g : 32 * g + 32, 128 * f : 128 * f + 128] for f in range(4)], axis=0
             )
-            cells = jnp.dot(pick[0], cells, preferred_element_type=F32).astype(BF16)
-            away[pl.ds(block * (QB // 2) + 8 * g, 8)] = cells.reshape(8, 16, 128)
+            cells = jnp.dot(pick[0], cells, preferred_element_type=F32)
+            away[i, pl.ds(block * (QB // 2) + 16 * g, 16)] = cells.reshape(16, 8, 128).astype(BF16)
 
         def send(k, n):
             to_chip = lax.rem(chip + k, ROWS // 2)
             turn = lax.rem(c + n, 4)
             to = (2 * to_chip + to_core, 4 * part + turn)
-            src, dst = away.at[64 * block + 16 * turn + to_chip], here.at[COLS * place + c]
+            src, dst = away.at[i, 64 * block + 16 * turn + to_chip], here.at[core, i, COLS * chip + c]
             return to, src, dst, pltpu.make_async_remote_copy(
                 src, dst, h_sent, h_sem.at[core], device_id=to, device_id_type=MESH
             )
@@ -171,17 +165,55 @@
             for n in range(4):
                 send(k, n)[-1].start()
 
-    for load in loads[2:]:
+    pl.semaphore_wait(met, 3)
+
+    @pl.loop(1, COLS)
+    def _(k):
+        pl.semaphore_signal(known, inc=1, device_id=(r, lax.rem(c + k, COLS)), device_id_type=MESH)
+
+    loads[0].wait()
+    loads[1].wait()
+    for i in range(2):
+        arrived(x1.at[i], x_sem.at[i])
+        if i == 0:
+
+            @pl.when(core == 0)
+            def _():
+                pl.semaphore_signal(go, inc=1, device_id=(r + 1, c), device_id_type=MESH)
+
+        project(x1[i].reshape(SEQ, D), g1[...], w1, q_ref, kt_ref, v_ref, i, 0, SEQ)
+        if i == 0:
+            loads[2].wait()
+            pl.semaphore_wait(known, COLS - 1)
+
+            @pl.loop(0, 2)
+            def _(step):
+                row_block(0, 0, lax.rem(step + chip, 2))
+
+    @pl.loop(0, 6)
+    def _(step):
+        turn = step // 2 + 1
+        row_block(lax.rem(turn, 2), turn // 2, lax.rem(step + chip, 2))
+
+    for load in loads[3:]:
         load.wait()
 
-    half = ROWS * COLS // 2
     for h in range(2):
-        arrived(here.at[pl.ds(half * h, half)], h_sem.at[h])
+        arrived(here.at[h], h_sem.at[h])
 
         @pl.loop(0, ROWS // 4)
         def _(n):
             first = ROWS // 2 * h + 2 * n
-            pair = [here[pl.ds((first + m) * COLS, COLS)].reshape(128, 128) for m in range(2)]
+            pair = [
+                jnp.concatenate(
+                    [
+                        here[h, i, pl.ds((2 * n + m) * COLS, COLS)].astype(F32).reshape(64, 128).astype(BF16)
+                        for i in range(2)
+                    ],
+                    axis=0,
+                )
+                for m in range(2)
+            ]
             cells = jnp.dot(pick[1], jnp.concatenate(pair, axis=1), preferred_element_type=F32).astype(BF16)
             for m in range(2):
                 for f in range(4):
@@ -192,7 +224,7 @@
 
         for j in range(2):
             n = SEQ // 2
-            project(x2[j, n * h : n * h + n], gain_lat[...], w2, q_ref, kt_ref, v_ref, j, n * h, n)
+            project(x2[j, n * h : n * h + n], g2[...], w2, q_ref, kt_ref, v_ref, j, n * h, n)
 
     for j in range(2):
 
@@ -241,24 +273,25 @@
 
     for i in range(2):
         arrived(x1.at[i, :, pl.ds(0, COLS - 1)], x_sent.at[i])
-    arrived(away.at[pl.ds(0, ROWS * COLS - 1)], h_sent)
+    arrived(away.at[:, pl.ds(0, ROWS * COLS - 1)], h_sent)
     arrived(back.at[pl.ds(0, 2 * (ROWS - 1))], b_sent)
     for out in outs:
         out.wait()
 
 
 def per_device(grid, gain_lon, qkv_lon, out_lon, gain_lat, qkv_lat, out_lat):
-    place = pl.BlockSpec(memory_space=pl.ANY)
-    whole = pl.BlockSpec(memory_space=pltpu.VMEM)
+    place = pl.BlockSpec(memory_space=pltpu.HBM)
     dma = pltpu.SemaphoreType.DMA
     return pl.pallas_call(
         kernel,
         out_shape=jax.ShapeDtypeStruct((16, 64, D), BF16),
-        in_specs=[place, whole, place, place, whole, place, place],
-        out_specs=place,
+        in_specs=[place] * 7,
+        out_specs=pl.BlockSpec(memory_space=pl.ANY),
         scratch_shapes=[
+            pltpu.VMEM((1, D), F32),
             pltpu.VMEM((D, 3 * D), BF16),
             pltpu.VMEM((D, D), BF16),
+            pltpu.VMEM((1, D), F32),
             pltpu.VMEM((D, 3 * D), BF16),
             pltpu.VMEM((D, D), BF16),
             pltpu.VMEM((2, 2, COLS, 32, D), BF16),
@@ -268,14 +301,16 @@
             pltpu.VMEM((2, PAIRS, 2 * SEQ, 256), BF16),
             pltpu.VMEM((2, 128, 128), BF16),
             pltpu.VMEM((256, 256), BF16),
-            pltpu.VMEM((ROWS * COLS, 16, 128), BF16),
-            pltpu.VMEM((ROWS * COLS, 16, 128), BF16),
+            pltpu.VMEM((2, ROWS * COLS, 8, 128), BF16),
+            pltpu.VMEM((2, 2, ROWS * COLS // 2, 8, 128), BF16),
             pltpu.VMEM((2, SEQ, D), BF16),
             pltpu.VMEM((64, 16, D), BF16),
             pltpu.VMEM((16, 64, D), BF16),
-            dma((4,)),
+            dma((6,)),
             dma((2,)),
             dma((2,)),
+            pltpu.SemaphoreType.REGULAR,
+            pltpu.SemaphoreType.REGULAR,
             pltpu.SemaphoreType.REGULAR,
             dma((2,)),
             dma,
@@ -284,7 +319,7 @@
             dma((4,)),
         ],
         compiler_params=pltpu.CompilerParams(
-            collective_id=0, has_side_effects=True, vmem_limit_bytes=48 * 2**20
+            collective_id=0, has_side_effects=True, vmem_limit_bytes=56 * 2**20
         ),
         cost_estimate=pl.CostEstimate(flops=6 * 10**9, bytes_accessed=8 * 2**20, transcendentals=8 * 2**20),
     )(grid.reshape(16, 2, 32, D), gain_lon.reshape(1, D), qkv_lon, out_lon, gain_lat.reshape(1, D), qkv_lat, out_lat)

time: 86.2 us -> 76.8 us (0.89)
  local copies, waits for them, and re-layouts: 7.05 us -> 2.29 us
  Pallas kernels: 78.8 us -> 74.4 us
    unnamed x13 -> x1, local copies, waits for them, and re-layouts: 7.05 us -> 2.29 us
    pallas_call x1, Pallas kernels: 78.8 us -> 74.4 us  [per_device(): pl.pallas_call(kernel, out_shape=jax.ShapeDtypeStruct((16, 64, D), BF16),...]
where the time goes in v3:
time: 76.8 us; the launch traced here: 76.7 us
  Pallas kernels  74.4 us (97%)
  local copies, waits for them, and re-layouts  2.29 us (3%)
    pallas_call x1, Pallas kernels, per_device(): pl.pallas_call(kernel, out_shape=jax.ShapeDtypeStruct((16, 64, D), BF16),...  74.4 us
    unnamed x1, local copies, waits for them, and re-layouts  2.29 us

profile of v3, /device:TPU:1, one launch (start us, length us, event | category | flops | bytes accessed | tf_op | source)
XLA Modules:
  0.0 76.7 jit_solution(13171945029087164400)
XLA Ops:
  0.0 74.4 %shard_map.73 = bf16[16,64,512]{2,1,0:T(8,128)(2,1)} custom-call(bf16[16,2,32,512]{3,2,1,0:T(8,128)(2,1)} %bitcast.3, f32[1,512]{1,0:T(1,128)} %bitcast.4, bf16[512,1536]{1,0:T(8,128)(2,1)} %qkv_lon.1, bf16[512,512]{1,0:T(8,128)(2,1)} %out_lon.1, f32[1,512]{1,0:T(1,128)} %bitcast.5, bf16[512,1536]{1,0:T(8,128)(2,1)} %qkv_lat.1, bf16[512,512]{1,0:T(8,128)(2,1)} %out_lat.1), custom_call_target="tpu_custom_call" | custom-call | flops 6000000000 | bytes 8388608 | tf_op jit(solution)/shard_map/pallas_call | solution.py:285
  74.4 2.3 %copy.9 = bf16[16,64,512]{2,1,0:T(8,128)(2,1)} copy(bf16[16,64,512]{2,1,0:T(8,128)(2,1)} %shard_map.73) | data formatting | bytes 2097152

commit v4 on v3

--- a/solution.py
+++ b/solution.py
@@ -65,7 +65,7 @@
 def kernel(
     grid_ref, gain_lon, qkv_lon, out_lon, gain_lat, qkv_lat, out_lat, result_ref,
     g1, w1, o1, g2, w2, o2, x1, x2, q_ref, kt_ref, v_ref, pick, pick3, away, here, done, back, final,
-    w_sem, x_sem, x_sent, go, met, known, h_sem, h_sent, b_sem, b_sent, f_sem,
+    w_sem, x_sem, x_sent, met, known, h_sem, h_sent, b_sem, b_sent, f_sem,
 ):
     r, c = lax.axis_index("rows"), lax.axis_index("cols")
     core, chip = lax.rem(r, 2), r // 2
@@ -111,19 +111,17 @@
     for i in range(2):
         pltpu.make_async_copy(grid_ref.at[2 * c + i], x1.at[i, :, c], x_sem.at[i]).start()
 
-    @pl.when(core == 1)
-    def _():
-        pl.semaphore_wait(go, 1)
-
-    for i in range(2):
-
-        @pl.loop(1, COLS)
-        def _(k):
-            to = lax.rem(c + k, COLS)
-            pltpu.make_async_remote_copy(
-                grid_ref.at[2 * to + i], x1.at[i, :, c], x_sent.at[i], x_sem.at[i],
-                device_id=(r, to), device_id_type=MESH,
-            ).start()
+    def piece(i, h, q, k):
+        to, cells = lax.rem(c + k, COLS), pl.ds(16 * q, 16)
+        pltpu.make_async_remote_copy(
+            grid_ref.at[2 * to + i, h, cells], x1.at[i, h, c, cells], x_sent.at[i], x_sem.at[i],
+            device_id=(r, to), device_id_type=MESH,
+        ).start()
+
+    for i, h in ((0, 0), (0, 1), (1, 0), (1, 1)):
+        for q in range(2):
+            for k in (1, 7, 2, 6, 3, 5, 4):
+                piece(i, h, q, k)
 
     def row_block(i, to_core, part):
         block = 2 * to_core + part
@@ -160,10 +158,15 @@
             def _():
                 copy.start()
 
-        @pl.loop(1, ROWS // 2)
+        @pl.loop(1, 8)
         def _(k):
             for n in range(4):
                 send(k, n)[-1].start()
+            for n in range(4):
+                send(16 - k, n)[-1].start()
+
+        for n in range(4):
+            send(8, n)[-1].start()
 
     pl.semaphore_wait(met, 3)
 
@@ -175,12 +178,6 @@
     loads[1].wait()
     for i in range(2):
         arrived(x1.at[i], x_sem.at[i])
-        if i == 0:
-
-            @pl.when(core == 0)
-            def _():
-                pl.semaphore_signal(go, inc=1, device_id=(r + 1, c), device_id_type=MESH)
-
         project(x1[i].reshape(SEQ, D), g1[...], w1, q_ref, kt_ref, v_ref, i, 0, SEQ)
         if i == 0:
             loads[2].wait()
@@ -222,11 +219,14 @@
                             32 * f + 16 * j : 32 * f + 16 * j + 16, 128 * m : 128 * m + 128
                         ]
 
-        for j in range(2):
+        for j in range(2 - h):
             n = SEQ // 2
             project(x2[j, n * h : n * h + n], g2[...], w2, q_ref, kt_ref, v_ref, j, n * h, n)
 
     for j in range(2):
+        if j == 1:
+            n = SEQ // 2
+            project(x2[j, n:], g2[...], w2, q_ref, kt_ref, v_ref, j, n, n)
 
         @pl.loop(0, SEQ // QB)
         def _(step):
@@ -254,8 +254,7 @@
             def _():
                 copy.start()
 
-            @pl.loop(1, QB // 16)
-            def _(k):
+            for k in (1, 7, 2, 6, 3, 5, 4):
                 send(k)[-1].start()
 
     outs = []
@@ -311,7 +310,6 @@
             dma((2,)),
             pltpu.SemaphoreType.REGULAR,
             pltpu.SemaphoreType.REGULAR,
-            pltpu.SemaphoreType.REGULAR,
             dma((2,)),
             dma,
             dma((4,)),

time: 76.8 us -> 75.1 us (0.978)
  Pallas kernels: 74.4 us -> 72.7 us
    pallas_call x1, Pallas kernels: 74.4 us -> 72.7 us  [per_device(): pl.pallas_call(kernel, out_shape=jax.ShapeDtypeStruct((16, 64, D), BF16),...]
where the time goes in v4:
time: 75.1 us; the launch traced here: 75 us
  Pallas kernels  72.7 us (97%)
  local copies, waits for them, and re-layouts  2.29 us (3%)
    pallas_call x1, Pallas kernels, per_device(): pl.pallas_call(kernel, out_shape=jax.ShapeDtypeStruct((16, 64, D), BF16),...  72.7 us
    unnamed x1, local copies, waits for them, and re-layouts  2.29 us

profile of v4, /device:TPU:1, one launch (start us, length us, event | category | flops | bytes accessed | tf_op | source)
XLA Modules:
  0.0 75.0 jit_solution(1323478680485461962)
XLA Ops:
  0.0 72.7 %shard_map.73 = bf16[16,64,512]{2,1,0:T(8,128)(2,1)} custom-call(bf16[16,2,32,512]{3,2,1,0:T(8,128)(2,1)} %bitcast.3, f32[1,512]{1,0:T(1,128)} %bitcast.4, bf16[512,1536]{1,0:T(8,128)(2,1)} %qkv_lon.1, bf16[512,512]{1,0:T(8,128)(2,1)} %out_lon.1, f32[1,512]{1,0:T(1,128)} %bitcast.5, bf16[512,1536]{1,0:T(8,128)(2,1)} %qkv_lat.1, bf16[512,512]{1,0:T(8,128)(2,1)} %out_lat.1), custom_call_target="tpu_custom_call" | custom-call | flops 6000000000 | bytes 8388608 | tf_op jit(solution)/shard_map/pallas_call | solution.py:284
  72.7 2.3 %copy.9 = bf16[16,64,512]{2,1,0:T(8,128)(2,1)} copy(bf16[16,64,512]{2,1,0:T(8,128)(2,1)} %shard_map.73) | data formatting | bytes 2097152

commit v5 on v4

--- a/solution.py
+++ b/solution.py
@@ -109,12 +109,13 @@
         pl.semaphore_signal(met, inc=1, device_id=(to, c), device_id_type=MESH)
 
     for i in range(2):
-        pltpu.make_async_copy(grid_ref.at[2 * c + i], x1.at[i, :, c], x_sem.at[i]).start()
+        for h in range(2):
+            pltpu.make_async_copy(grid_ref.at[2 * c + i, h], x1.at[i, h, c], x_sem.at[2 * i + h]).start()
 
     def piece(i, h, q, k):
         to, cells = lax.rem(c + k, COLS), pl.ds(16 * q, 16)
         pltpu.make_async_remote_copy(
-            grid_ref.at[2 * to + i, h, cells], x1.at[i, h, c, cells], x_sent.at[i], x_sem.at[i],
+            grid_ref.at[2 * to + i, h, cells], x1.at[i, h, c, cells], x_sent.at[i], x_sem.at[2 * i + h],
             device_id=(r, to), device_id_type=MESH,
         ).start()
 
@@ -135,18 +136,26 @@
                 [first[32 * g : 32 * g + 32, 128 * f : 128 * f + 128] for f in range(4)], axis=0
             )
             cells = jnp.dot(pick[0], cells, preferred_element_type=F32)
-            away[i, pl.ds(block * (QB // 2) + 16 * g, 16)] = cells.reshape(16, 8, 128).astype(BF16)
+            away[pl.ds(block * (QB // 2) + 16 * g, 16), i] = cells.reshape(16, 8, 128).astype(BF16)
+
+    def send_block(to_core, part, i):
+        block = 2 * to_core + part
 
         def send(k, n):
             to_chip = lax.rem(chip + k, ROWS // 2)
             turn = lax.rem(c + n, 4)
             to = (2 * to_chip + to_core, 4 * part + turn)
-            src, dst = away.at[i, 64 * block + 16 * turn + to_chip], here.at[core, i, COLS * chip + c]
+            src, dst = away.at[64 * block + 16 * turn + to_chip], here.at[core, COLS * chip + c]
+            if i is not None:
+                src, dst = src.at[i], dst.at[i]
             return to, src, dst, pltpu.make_async_remote_copy(
                 src, dst, h_sent, h_sem.at[core], device_id=to, device_id_type=MESH
             )
 
-        for n in range(4):
+        @pl.loop(0, 4)
+        def _(n):
+            for k in (4, 12, 3, 13, 5, 11, 2, 14, 6, 10, 1, 15, 7, 9, 8):
+                send(k, n)[-1].start()
             to, src, dst, copy = send(0, n)
             own = jnp.logical_and(to[0] == r, to[1] == c)
 
@@ -158,16 +167,6 @@
             def _():
                 copy.start()
 
-        @pl.loop(1, 8)
-        def _(k):
-            for n in range(4):
-                send(k, n)[-1].start()
-            for n in range(4):
-                send(16 - k, n)[-1].start()
-
-        for n in range(4):
-            send(8, n)[-1].start()
-
     pl.semaphore_wait(met, 3)
 
     @pl.loop(1, COLS)
@@ -177,20 +176,35 @@
     loads[0].wait()
     loads[1].wait()
     for i in range(2):
-        arrived(x1.at[i], x_sem.at[i])
-        project(x1[i].reshape(SEQ, D), g1[...], w1, q_ref, kt_ref, v_ref, i, 0, SEQ)
+        for h in range(2):
+            arrived(x1.at[i, h], x_sem.at[2 * i + h])
+            n = SEQ // 2
+            project(x1[i, h].reshape(n, D), g1[...], w1, q_ref, kt_ref, v_ref, i, n * h, n)
         if i == 0:
             loads[2].wait()
             pl.semaphore_wait(known, COLS - 1)
 
             @pl.loop(0, 2)
             def _(step):
-                row_block(0, 0, lax.rem(step + chip, 2))
-
-    @pl.loop(0, 6)
+                part = lax.rem(step + chip, 2)
+                row_block(0, 0, part)
+                send_block(0, part, 0)
+
+    @pl.loop(0, 2)
     def _(step):
-        turn = step // 2 + 1
-        row_block(lax.rem(turn, 2), turn // 2, lax.rem(step + chip, 2))
+        part = lax.rem(step + chip, 2)
+        row_block(1, 0, part)
+        send_block(0, part, 1)
+
+    @pl.loop(0, 2)
+    def _(step):
+        part = lax.rem(step + chip, 2)
+
+        @pl.loop(0, 2)
+        def _(i):
+            row_block(i, 1, part)
+
+        send_block(1, part, None)
 
     for load in loads[3:]:
         load.wait()
@@ -204,7 +218,7 @@
             pair = [
                 jnp.concatenate(
                     [
-                        here[h, i, pl.ds((2 * n + m) * COLS, COLS)].astype(F32).reshape(64, 128).astype(BF16)
+                        here[h, pl.ds((2 * n + m) * COLS, COLS), i].astype(F32).reshape(64, 128).astype(BF16)
                         for i in range(2)
                     ],
                     axis=0,
@@ -272,7 +286,7 @@
 
     for i in range(2):
         arrived(x1.at[i, :, pl.ds(0, COLS - 1)], x_sent.at[i])
-    arrived(away.at[:, pl.ds(0, ROWS * COLS - 1)], h_sent)
+    arrived(away.at[pl.ds(0, ROWS * COLS - 1)], h_sent)
     arrived(back.at[pl.ds(0, 2 * (ROWS - 1))], b_sent)
     for out in outs:
         out.wait()
@@ -300,13 +314,13 @@
             pltpu.VMEM((2, PAIRS, 2 * SEQ, 256), BF16),
             pltpu.VMEM((2, 128, 128), BF16),
             pltpu.VMEM((256, 256), BF16),
-            pltpu.VMEM((2, ROWS * COLS, 8, 128), BF16),
-            pltpu.VMEM((2, 2, ROWS * COLS // 2, 8, 128), BF16),
+            pltpu.VMEM((ROWS * COLS, 2, 8, 128), BF16),
+            pltpu.VMEM((2, ROWS * COLS // 2, 2, 8, 128), BF16),
             pltpu.VMEM((2, SEQ, D), BF16),
             pltpu.VMEM((64, 16, D), BF16),
             pltpu.VMEM((16, 64, D), BF16),
             dma((6,)),
-            dma((2,)),
+            dma((4,)),
             dma((2,)),
             pltpu.SemaphoreType.REGULAR,
             pltpu.SemaphoreType.REGULAR,

time: 75.1 us -> 73.4 us (0.977)
  Pallas kernels: 72.7 us -> 71 us
    pallas_call x1, Pallas kernels: 72.7 us -> 71 us  [per_device(): pl.pallas_call(kernel, out_shape=jax.ShapeDtypeStruct((16, 64, D), BF16),...]
where the time goes in v5:
time: 73.4 us; the launch traced here: 73.3 us
  Pallas kernels  71 us (97%)
  local copies, waits for them, and re-layouts  2.29 us (3%)
    pallas_call x1, Pallas kernels, per_device(): pl.pallas_call(kernel, out_shape=jax.ShapeDtypeStruct((16, 64, D), BF16),...  71 us
    unnamed x1, local copies, waits for them, and re-layouts  2.29 us

profile of v5, /device:TPU:1, one launch (start us, length us, event | category | flops | bytes accessed | tf_op | source)
XLA Modules:
  0.0 73.3 jit_solution(17437345561965462809)
XLA Ops:
  0.0 71.0 %shard_map.73 = bf16[16,64,512]{2,1,0:T(8,128)(2,1)} custom-call(bf16[16,2,32,512]{3,2,1,0:T(8,128)(2,1)} %bitcast.3, f32[1,512]{1,0:T(1,128)} %bitcast.4, bf16[512,1536]{1,0:T(8,128)(2,1)} %qkv_lon.1, bf16[512,512]{1,0:T(8,128)(2,1)} %out_lon.1, f32[1,512]{1,0:T(1,128)} %bitcast.5, bf16[512,1536]{1,0:T(8,128)(2,1)} %qkv_lat.1, bf16[512,512]{1,0:T(8,128)(2,1)} %out_lat.1), custom_call_target="tpu_custom_call" | custom-call | flops 6000000000 | bytes 8388608 | tf_op jit(solution)/shard_map/pallas_call | solution.py:298
  71.0 2.3 %copy.9 = bf16[16,64,512]{2,1,0:T(8,128)(2,1)} copy(bf16[16,64,512]{2,1,0:T(8,128)(2,1)} %shard_map.73) | data formatting | bytes 2097152

commit v6 on v5

--- a/solution.py
+++ b/solution.py
@@ -268,7 +268,7 @@
             def _():
                 copy.start()
 
-            for k in (1, 7, 2, 6, 3, 5, 4):
+            for k in (4, 3, 5, 2, 6, 1, 7):
                 send(k)[-1].start()
 
     outs = []

time: 73.4 us -> 73.1 us (level)
  no operation moved by 1% of the time
where the time goes in v6:
time: 73.1 us; the launch traced here: 73 us
  Pallas kernels  70.7 us (97%)
  local copies, waits for them, and re-layouts  2.29 us (3%)
    pallas_call x1, Pallas kernels, per_device(): pl.pallas_call(kernel, out_shape=jax.ShapeDtypeStruct((16, 64, D), BF16),...  70.7 us
    unnamed x1, local copies, waits for them, and re-layouts  2.29 us

profile of v6, /device:TPU:1, one launch (start us, length us, event | category | flops | bytes accessed | tf_op | source)
XLA Modules:
  0.0 73.0 jit_solution(14879318236738707239)
XLA Ops:
  0.0 70.7 %shard_map.73 = bf16[16,64,512]{2,1,0:T(8,128)(2,1)} custom-call(bf16[16,2,32,512]{3,2,1,0:T(8,128)(2,1)} %bitcast.3, f32[1,512]{1,0:T(1,128)} %bitcast.4, bf16[512,1536]{1,0:T(8,128)(2,1)} %qkv_lon.1, bf16[512,512]{1,0:T(8,128)(2,1)} %out_lon.1, f32[1,512]{1,0:T(1,128)} %bitcast.5, bf16[512,1536]{1,0:T(8,128)(2,1)} %qkv_lat.1, bf16[512,512]{1,0:T(8,128)(2,1)} %out_lat.1), custom_call_target="tpu_custom_call" | custom-call | flops 6000000000 | bytes 8388608 | tf_op jit(solution)/shard_map/pallas_call | solution.py:298
  70.7 2.3 %copy.9 = bf16[16,64,512]{2,1,0:T(8,128)(2,1)} copy(bf16[16,64,512]{2,1,0:T(8,128)(2,1)} %shard_map.73) | data formatting | bytes 2097152
